TPU v7x, 256 devices: a whole 4x4x8 slice. The times are simulated.
256 devices in a mesh: grp: 8 (over x, core), dev: 32 (over y, z).
Axes of the slice: x: 4, y: 4, z: 8, core: 2. Of those that a mesh axis runs over, the one named last changes fastest.
Arguments:
- sources: bfloat16 [4, 524288], P(None, ('grp', 'dev')), may hold values from -6 to 6
- self_near_block: bfloat16 [1024, 512, 512], P(('grp', 'dev')), may hold values from -0.1875 to 0.1875
- neighbour_near_block: bfloat16 [1024, 512, 512], P(('grp', 'dev')), may hold values from -0.1875 to 0.1875
- near_list: int32 [1024], P(('grp', 'dev')), may hold values from 0 to 1023, as said below
- bases: bfloat16 [1024, 64, 512], P(('grp', 'dev')), may hold values from -0.25 to 0.25
- far_leaf: int32 [1024, 16], P(('grp', 'dev')), may hold values from 0 to 1023, as said below
- far_count: int32 [1024], P(('grp', 'dev')), may hold values from 1 to 16, 8192 in all
- leaf_coupling: float32 [1024, 16, 64, 64], P(('grp', 'dev')), may hold values from -0.375 to 0.375
- leaf_transfer: float32 [1024, 64, 64], P(('grp', 'dev')), may hold values from -0.5 to 0.5
- far_cluster: int32 [256, 8], P(('grp', 'dev')), may hold values from 0 to 255, as said below
- cluster_coupling: float32 [256, 8, 64, 64], P(('grp', 'dev')), may hold values from -0.375 to 0.375
- cluster_transfer: float32 [256, 64, 64], P(('grp', 'dev')), may hold values from -0.375 to 0.375
- top_coupling: float32 [8, 8, 64, 64], P('grp'), may hold values from -0.375 to 0.375
Outputs:
- potential: float32 [4, 524288], P(None, ('grp', 'dev'))
Inputs may be any that keep to these rules, and one draw needn't show every extreme that they name: near_list names a leaf held by the same device as the leaf or by one of the two devices beside it in the order of grp then dev. far_leaf names a leaf held by a device 2 to 3 places away from the leaf's own device in the order of grp then dev. far_cluster names a device cluster of the same group cluster as the row's own, never the row's own. Slots from far_count on are ignored.
All inputs are finite; a program needn't handle non-finite values. No bound on the sum of `far_count` on one device may be relied on, other than what follows from the above.
Results may differ from a plain program's by a relative error of at most 0.00045.
Values may be sent and summed in bfloat16 or wider, within the bound.
No kernel may reach another device: no remote copies, remote signals or barrier semaphores. Data moves between devices by JAX's collectives and lax.ppermute only.
A program may use at most 64 MiB of HBM per device.

v0:
```python
import jax
import jax.numpy as jnp
from jax import lax
from jax.experimental import pallas as pl
from jax.experimental.pallas import tpu as pltpu
from jax.sharding import PartitionSpec as P

HIGH = lax.Precision.HIGHEST
F32 = jnp.float32
BF16 = jnp.bfloat16
LEAF = 512
RANK = 64
NVEC = 4
LPD = 4
FARW = 3
TURN = 31
WIDE = LPD * RANK
VMEM = pl.BlockSpec(memory_space=pltpu.VMEM)
HBM = pl.BlockSpec(memory_space=pltpu.HBM)
SMEM = pl.BlockSpec(memory_space=pltpu.SMEM)


def rows_by_rows(a, b, precision=None):
    return lax.dot_general(
        a, b, (((1,), (1,)), ((), ())), precision=precision, preferred_element_type=F32
    )


def exact_dot(a, b):
    return jnp.dot(a, b, precision=HIGH, preferred_element_type=F32)


def parts_of(rows):
    high = rows.astype(BF16).astype(F32)
    middle = (rows - high).astype(BF16).astype(F32)
    low = rows - high - middle
    return jnp.concatenate([high, middle, low, jnp.zeros_like(low)], axis=0).astype(BF16)


def two_parts(matrix):
    high = matrix.astype(BF16)
    return high, (matrix - high.astype(F32)).astype(BF16)


def close_dot(rows, matrix):
    parts = parts_of(rows)
    out = jnp.dot(parts, matrix[0], preferred_element_type=F32)
    small = jnp.dot(parts[:16], matrix[1], preferred_element_type=F32)
    return out[:8] + (out[8:16] + small[:8]) + (out[16:24] + small[8:16])


def tiles(matrix):
    return matrix.reshape(RANK // 8, 8, RANK)


def no_sums():
    return [jnp.zeros((RANK // 8, 8, RANK), F32) for _ in range(NVEC)]


def lanes_to_matrix(sums):
    lane = lax.broadcasted_iota(jnp.int32, (RANK, 128), 1)
    out = jnp.zeros((RANK, 128), F32)
    for v, s in enumerate(sums):
        column = jnp.sum(s, axis=-1, keepdims=True).reshape(RANK, 1)
        out = jnp.where(lane == v, column, out)
    return out


def spread(rows, v):
    return jnp.broadcast_to(rows[v : v + 1], (8, RANK))


def up_kernel(
    src_h, bases_h, leaf_h, cluster_h, send, src, bases, leaf, cluster, sem
):
    copies = [
        pltpu.make_async_copy(a, b, sem.at[i])
        for i, (a, b) in enumerate(
            (
                (leaf_h, leaf),
                (cluster_h, cluster),
                (src_h, src),
                (bases_h, bases),
            )
        )
    ]
    for c in copies:
        c.start()
    copies[0].wait()
    copies[1].wait()
    to_cluster = two_parts(leaf[...].reshape(WIDE, RANK))
    to_group = two_parts(cluster[0])
    copies[2].wait()
    copies[3].wait()
    every = jnp.concatenate(
        [rows_by_rows(src[:, l * LEAF : (l + 1) * LEAF], bases[l]) for l in range(LPD)], axis=1
    )
    cluster_rows = close_dot(jnp.concatenate([every, jnp.zeros_like(every)], axis=0), to_cluster)
    group_rows = close_dot(cluster_rows, to_group)
    row = jnp.concatenate([cluster_rows[:NVEC], group_rows[:NVEC], every], axis=1)
    for i in range(send.shape[0]):
        send[i] = row


def own_kernel(src, self_h, other_h, own, other, block, sem):
    copies = [
        pltpu.make_async_copy(self_h.at[l], block.at[l], sem.at[l]) for l in range(LPD)
    ] + [pltpu.make_async_copy(other_h, other, sem.at[LPD])]
    for c in copies:
        c.start()
    for l in range(LPD):
        at = slice(l * LEAF, (l + 1) * LEAF)
        copies[l].wait()
        own[:, at] = rows_by_rows(src[:, at], block[l])
    copies[LPD].wait()


def near_kernel(near_list, src, even_swap, odd_swap, own, other, near):
    me = lax.axis_index("grp") * lax.axis_size("dev") + lax.axis_index("dev")
    is_odd = (me & 1) == 1
    for l in range(LPD):
        here = jnp.clip(near_list[l] - me * LPD + LPD, 0, 3 * LPD - 1)
        at = pl.multiple_of((here & (LPD - 1)) * LEAF, LEAF)
        which = here >> 2
        x1 = src[:, pl.ds(at, LEAF)]
        x2 = odd_swap[:, pl.ds(at, LEAF)]
        x3 = even_swap[:, pl.ds(at, LEAF)]
        x = jnp.where(which == 1, x1, jnp.where((which == 0) == is_odd, x2, x3))
        at = slice(l * LEAF, (l + 1) * LEAF)
        near[:, at] = own[:, at] + rows_by_rows(x, other[l])


def group_kernel(first, send):
    d = lax.axis_index("dev")
    n_dev = first.shape[0]
    total = jnp.sum(first[:, :, : 2 * RANK], axis=0)
    low = d < FARW
    a = jnp.where(low, jnp.minimum(n_dev - FARW + d, n_dev - 1), jnp.maximum(d - (n_dev - 2), 0))
    b = jnp.where(
        low, jnp.minimum(n_dev - FARW + 1 + d, n_dev - 1), jnp.maximum(d - (n_dev - FARW), 0)
    )
    a, b = (a - TURN) & (n_dev - 1), (b - TURN) & (n_dev - 1)
    row = jnp.concatenate([total, first[a, :, 2 * RANK :], first[b, :, 2 * RANK :]], axis=1)
    for i in range(send.shape[0]):
        send[i] = row


def far_sums(coupling, l, table, entry):
    sums = no_sums()
    for s in range(coupling.shape[1]):
        c = tiles(coupling[l, s])
        at = entry(l, s)
        for v in range(NVEC):
            sums[v] = sums[v] + c * table[at, v][None]
    return lanes_to_matrix(sums)


def fill(table, first_entry, value):
    for l in range(LPD):
        for v in range(NVEC):
            table[first_entry + l, v] = spread(value[:, l * RANK : (l + 1) * RANK], v)


def mid_kernel(
    far_leaf, far_count, far_cluster, first, near, leaf_h, transfer_h, bases_h, coupling_h,
    cluster_h, top_h, base, down_high, down_low, bases, coupling, top_out, leaf_transfer, transfer,
    cluster, table, sem
):
    copies = []
    for a, b in (
        [(leaf_h, leaf_transfer), (transfer_h, transfer), (cluster_h, cluster)]
        + [(bases_h, bases)]
        + [(coupling_h.at[l], coupling.at[l]) for l in range(LPD)]
        + [(top_h, top_out)]
    ):
        copy = pltpu.make_async_copy(a, b, sem.at[len(copies)])
        copy.start()
        copies.append(copy)
    d = lax.axis_index("dev")
    n_dev = lax.axis_size("dev")
    me = lax.axis_index("grp") * n_dev + d

    for pos, off in enumerate((-3, -2, 2, 3)):
        fill(table, pos * LPD, first[(d + off - TURN) & (n_dev - 1), :, 2 * RANK :])
    table[4 * LPD] = jnp.zeros((NVEC, 8, RANK), F32)

    for c in copies[:3]:
        c.wait()
    to_cluster = leaf_transfer[...].reshape(WIDE, RANK)
    to_group = exact_dot(to_cluster, transfer[0])
    high = to_group.astype(BF16)
    down_high[...] = high
    down_low[...] = (to_group - high.astype(F32)).astype(BF16)
    sums = no_sums()
    for s in range(far_cluster.shape[1]):
        c = tiles(cluster[0, s])
        x = first[(far_cluster[0, s] - TURN) & (n_dev - 1), :, :RANK]
        for v in range(NVEC):
            sums[v] = sums[v] + c * spread(x, v)[None]
    from_cluster = exact_dot(to_cluster, lanes_to_matrix(sums))

    def entry(l, s):
        leaf = far_leaf[l, s]
        delta = (leaf >> 2) - me
        pos = jnp.where(delta < 0, delta + FARW, delta)
        here = jnp.logical_and(d + delta >= 0, d + delta < n_dev)
        live = jnp.logical_and(s < far_count[l], here)
        return jnp.clip(jnp.where(live, pos * LPD + (leaf & (LPD - 1)), 4 * LPD), 0, 4 * LPD)

    copies[3].wait()
    for l in range(LPD):
        copies[4 + l].wait()
        field = far_sums(coupling, l, table, entry) + from_cluster[l * RANK : (l + 1) * RANK]
        product = jnp.dot(
            parts_of(jnp.transpose(field)[:8]), bases[l], preferred_element_type=F32
        )
        product = product[:8] + product[8:16] + product[16:24]
        at = slice(l * LEAF, (l + 1) * LEAF)
        base[:, at] = near[:, at] + product[:NVEC]
    copies[4 + LPD].wait()


def down_kernel(
    far_leaf, far_count, base, down_high, down_low, bases, coupling, top_coupling, second, out,
    table
):
    g = lax.axis_index("grp")
    d = lax.axis_index("dev")
    n_dev = lax.axis_size("dev")
    n_grp = second.shape[0]
    me = g * n_dev + d

    sums = no_sums()
    for h in range(n_grp):
        c = tiles(top_coupling[0, h])
        x = jnp.where(h != g, second[h, :, RANK : 2 * RANK], 0.0)
        for v in range(NVEC):
            sums[v] = sums[v] + c * spread(x, v)[None]
    parts = parts_of(jnp.transpose(lanes_to_matrix(sums))[:8])
    field = rows_by_rows(parts, down_high[...])
    field = field[:8] + field[8:16] + field[16:24] + rows_by_rows(parts[:16], down_low[...])[:8]

    side = (g + jnp.where(d < FARW, -1, 1)) & (n_grp - 1)
    for k in range(2):
        start = 2 * RANK + k * WIDE
        fill(table, k * LPD, second[side, :, start : start + WIDE])
    table[2 * LPD] = jnp.zeros((NVEC, 8, RANK), F32)

    def entry(l, s):
        leaf = far_leaf[l, s]
        delta = (leaf >> 2) - me
        which = jnp.where(delta < 0, delta + FARW, delta) & 1
        there = jnp.logical_or(d + delta < 0, d + delta >= n_dev)
        live = jnp.logical_and(s < far_count[l], there)
        return jnp.where(live, which * LPD + (leaf & (LPD - 1)), 2 * LPD)

    for l in range(LPD):
        extra = jnp.transpose(far_sums(coupling, l, table, entry))[:8]
        parts = parts_of(field[:, l * RANK : (l + 1) * RANK] + extra)
        far = jnp.dot(parts, bases[l], preferred_element_type=F32)
        far = far[:8] + far[8:16] + far[16:24]
        at = slice(l * LEAF, (l + 1) * LEAF)
        out[:, at] = base[:, at] + far[:NVEC]


def permute(value, pairs):
    return lax.ppermute(value, ("grp", "dev"), pairs)


def swapped(value, start, count):
    pairs = [(i, (i + 1) % count) for i in range(start, count, 2)]
    return lax.ppermute(value, ("grp", "dev"), pairs + [(j, i) for i, j in pairs])


def in_hbm(*arrays):
    return [pltpu.with_memory_space_constraint(a, pltpu.HBM) for a in arrays]


def params(mib):
    return pltpu.CompilerParams(vmem_limit_bytes=mib * 1024 * 1024)


def cost(flops, size):
    return pl.CostEstimate(flops=flops, bytes_accessed=size, transcendentals=0)


def per_device(
    sources,
    self_near_block,
    neighbour_near_block,
    near_list,
    bases,
    far_leaf,
    far_count,
    leaf_coupling,
    leaf_transfer,
    far_cluster,
    cluster_coupling,
    cluster_transfer,
    top_coupling,
):
    n_dev = lax.axis_size("dev")
    n_grp = lax.axis_size("grp")
    n_all = n_dev * n_grp
    sds = jax.ShapeDtypeStruct
    send = pl.pallas_call(
        up_kernel,
        out_shape=sds((n_dev, NVEC, 2 * RANK + WIDE), F32),
        in_specs=[HBM] * 4,
        out_specs=VMEM,
        scratch_shapes=[
            pltpu.VMEM(sources.shape, BF16),
            pltpu.VMEM(bases.shape, BF16),
            pltpu.VMEM(leaf_transfer.shape, F32),
            pltpu.VMEM(cluster_transfer.shape, F32),
            pltpu.SemaphoreType.DMA((4,)),
        ],
        compiler_params=params(8),
        name="up",
    )(*in_hbm(sources, bases, leaf_transfer, cluster_transfer))
    turned = [(i + TURN) % n_dev for i in range(n_dev)]
    first = lax.all_to_all(send, "dev", 0, 0, axis_index_groups=[turned])
    send, tied = lax.optimization_barrier((send, sources))
    even_swap = swapped(tied, 1, n_all)
    odd_swap = swapped(tied, 0, n_all)
    own, other_v = pl.pallas_call(
        own_kernel,
        out_shape=[sds(sources.shape, F32), sds(neighbour_near_block.shape, BF16)],
        in_specs=[VMEM] + [HBM] * 2,
        out_specs=[VMEM] * 2,
        scratch_shapes=[
            pltpu.VMEM(self_near_block.shape, BF16),
            pltpu.SemaphoreType.DMA((1 + LPD,)),
        ],
        compiler_params=params(8),
        cost_estimate=cost(20000000, 4000000),
        name="own",
    )(*in_hbm(tied, self_near_block, neighbour_near_block))
    near = pl.pallas_call(
        near_kernel,
        out_shape=sds(sources.shape, F32),
        in_specs=[SMEM] + [VMEM] * 5,
        out_specs=VMEM,
        compiler_params=params(4),
        cost_estimate=cost(20000000, 2000000),
        name="near",
    )(*in_hbm(near_list, tied), even_swap, odd_swap, own, other_v)
    first, near = lax.optimization_barrier((first, near))
    send = pl.pallas_call(
        group_kernel,
        out_shape=sds((n_grp, NVEC, 2 * RANK + 2 * WIDE), F32),
        in_specs=[VMEM],
        out_specs=VMEM,
        compiler_params=params(4),
        name="group",
    )(first)
    second = lax.all_to_all(send, "grp", 0, 0)
    base, down_high, down_low, bases_v, coupling_v, top_v = pl.pallas_call(
        mid_kernel,
        out_shape=[
            sds(sources.shape, F32),
            sds((WIDE, RANK), BF16),
            sds((WIDE, RANK), BF16),
            sds(bases.shape, BF16),
            sds(leaf_coupling.shape, F32),
            sds(top_coupling.shape, F32),
        ],
        in_specs=[SMEM] * 3 + [VMEM] * 2 + [HBM] * 6,
        out_specs=[VMEM] * 6,
        scratch_shapes=[
            pltpu.VMEM(leaf_transfer.shape, F32),
            pltpu.VMEM(cluster_transfer.shape, F32),
            pltpu.VMEM(cluster_coupling.shape, F32),
            pltpu.VMEM((4 * LPD + 1, NVEC, 8, RANK), F32),
            pltpu.SemaphoreType.DMA((5 + LPD,)),
        ],
        compiler_params=params(12),
        cost_estimate=cost(40000000, 5000000),
        name="mid",
    )(
        *in_hbm(far_leaf, far_count, far_cluster),
        first,
        near,
        *in_hbm(
            leaf_transfer, cluster_transfer, bases, leaf_coupling, cluster_coupling, top_coupling
        ),
    )
    return pl.pallas_call(
        down_kernel,
        out_shape=sds(sources.shape, F32),
        in_specs=[SMEM] * 2 + [VMEM] * 7,
        out_specs=VMEM,
        scratch_shapes=[
            pltpu.VMEM((2 * LPD + 1, NVEC, 8, RANK), F32),
        ],
        compiler_params=params(8),
        name="down",
    )(
        *in_hbm(far_leaf, far_count),
        base,
        down_high,
        down_low,
        bases_v,
        coupling_v,
        top_v,
        second,
    )


def solution(mesh):
    placed = (
        P(None, ("grp", "dev")),
        P(("grp", "dev"), None, None),
        P(("grp", "dev"), None, None),
        P(("grp", "dev")),
        P(("grp", "dev"), None, None),
        P(("grp", "dev"), None),
        P(("grp", "dev")),
        P(("grp", "dev"), None, None, None),
        P(("grp", "dev"), None, None),
        P(("grp", "dev"), None),
        P(("grp", "dev"), None, None, None),
        P(("grp", "dev"), None, None),
        P("grp", None, None, None),
    )
    return jax.shard_map(
        per_device, mesh=mesh, in_specs=placed, out_specs=P(None, ("grp", "dev")), check_vma=False
    )
```

profile of v0, /device:TPU:1, one launch (start us, length us, event | category | flops | bytes accessed | tf_op | source)
XLA Modules:
  0.0 37.8 jit_solution(5508148922416328530)
XLA Ops:
  0.0 2.3 %up.1 = f32[32,4,384]{2,1,0:T(4,128)} custom-call(bf16[4,2048]{1,0:T(4,128)(2,1)} %src.1, bf16[4,64,512]{2,1,0:T(8,128)(2,1)} %bases_h.3, f32[4,64,64]{2,1,0:T(8,128)} %leaf_h.3, f32[1,64,64]{2,1,0:T(8,128)} %transfer_h.1), custom_call_target="tpu_custom_call" | custom-call | tf_op jit(solution)/shard_map/up/pallas_call | solution.py:306
  2.3 12.6 %all-to-all-start = ((f32[32,4,384]{2,1,0:T(4,128)}), f32[32,4,384]{2,1,0:T(4,128)S(1)}, u32[]{:S(2)}, u32[]{:S(2)}) async-start(f32[32,4,384]{2,1,0:T(4,128)} %up.1), calls=%async_computation | async-start | bytes 393216 | tf_op jit(solution)/shard_map/all_to_all | solution.py:322
  14.9 1.2 %collective-permute-start = (bf16[4,2048]{1,0:T(4,128)(2,1)}, bf16[4,2048]{1,0:T(4,128)(2,1)S(1)}, u32[]{:S(2)}, u32[]{:S(2)}) collective-permute-start(bf16[4,2048]{1,0:T(4,128)(2,1)} %src.1), channel_id=1, source_target_pairs={{1,2},{3,4},{5,6},{7,8},{9,10},{11,12},{13,14},{15,16},{17,18},{19... | collective-permute-start | bytes 49160 | tf_op jit(solution)/shard_map/ppermute | solution.py:272
  16.1 1.3 %collective-permute-start.1 = (bf16[4,2048]{1,0:T(4,128)(2,1)}, bf16[4,2048]{1,0:T(4,128)(2,1)S(1)}, u32[]{:S(2)}, u32[]{:S(2)}) collective-permute-start(bf16[4,2048]{1,0:T(4,128)(2,1)} %src.1), channel_id=1, source_target_pairs={{0,1},{2,3},{4,5},{6,7},{8,9},{10,11},{12,13},{14,15},{16,17},{18,... | collective-permute-start | bytes 49160 | tf_op jit(solution)/shard_map/ppermute | solution.py:272
  17.4 3.0 %own.1 = (f32[4,2048]{1,0:T(4,128)S(1)}, bf16[4,512,512]{2,1,0:T(8,128)(2,1)S(1)}) custom-call(bf16[4,2048]{1,0:T(4,128)(2,1)} %src.1, bf16[4,512,512]{2,1,0:T(8,128)(2,1)} %self_h.1, bf16[4,512,512]{2,1,0:T(8,128)(2,1)} %other_h.1), custom_call_target="tpu_custom_call" | custom-call | flops 20000000 | bytes 4000000 | tf_op jit(solution)/shard_map/own/pallas_call | solution.py:326
  20.4 1.6 %collective-permute-done.even_swap = bf16[4,2048]{1,0:T(4,128)(2,1)S(1)} collective-permute-done((bf16[4,2048]{1,0:T(4,128)(2,1)}, bf16[4,2048]{1,0:T(4,128)(2,1)S(1)}, u32[]{:S(2)}, u32[]{:S(2)}) %collective-permute-start) | collective-permute-done | bytes 16416 | tf_op jit(solution)/shard_map/ppermute | solution.py:272
  22.0 0.0 collective-permute-done.1.odd_swap
  22.0 1.4 %near.1 = f32[4,2048]{1,0:T(4,128)S(1)} custom-call(s32[4]{0:T(128)} %near_list.1, bf16[4,2048]{1,0:T(4,128)(2,1)} %src.1, bf16[4,2048]{1,0:T(4,128)(2,1)S(1)} %collective-permute-done.even_swap, bf16[4,2048]{1,0:T(4,128)(2,1)S(1)} %collective-permute-done.1.odd_swap, f32[4,2048]{1,0:T(4,128)S(1)} %get-tuple-element.17.own, ...), custom_call_target="tpu_custom_call" | custom-call | flops 20000000 | bytes 2000000 | tf_op jit(solution)/shard_map/near/pallas_call | solution.py:339
  23.4 0.0 all-to-all-done.first
  23.4 0.7 %group.1 = f32[8,4,640]{2,1,0:T(4,128)} custom-call(f32[32,4,384]{2,1,0:T(4,128)S(1)} %all-to-all-done.first), custom_call_target="tpu_custom_call" | custom-call | tf_op jit(solution)/shard_map/group/pallas_call | solution.py:349
  24.1 6.3 %all-to-all-start.1 = ((f32[8,4,640]{2,1,0:T(4,128)}), f32[8,4,640]{2,1,0:T(4,128)S(1)}, u32[]{:S(2)}, u32[]{:S(2)}) async-start(f32[8,4,640]{2,1,0:T(4,128)} %group.1), calls=%async_computation.1 | async-start | bytes 163840 | tf_op jit(solution)/shard_map/all_to_all | solution.py:357
  30.4 4.0 %mid.1 = (f32[4,2048]{1,0:T(4,128)S(1)}, bf16[256,64]{1,0:T(8,128)(2,1)S(1)}, bf16[256,64]{1,0:T(8,128)(2,1)S(1)}, bf16[4,64,512]{2,1,0:T(8,128)(2,1)S(1)}, f32[...) custom-call(s32[4,16]{1,0:T(4,128)} %far_leaf.3, s32[4]{0:T(128)} %far_count.3, s32[1,8]{1,0:T(1,128)} %far_cluster.1, ...), custom_call_target="tpu_custom_call" | custom-call | flops 40000000 | bytes 5000000 | tf_op jit(solution)/shard_map/mid/pallas_call | solution.py:358
  34.4 0.9 %all-to-all-done.1.second = f32[8,4,640]{2,1,0:T(4,128)S(1)} async-done(((f32[8,4,640]{2,1,0:T(4,128)}), f32[8,4,640]{2,1,0:T(4,128)S(1)}, u32[]{:S(2)}, u32[]{:S(2)}) %all-to-all-start.1) | async-done | bytes 81952 | tf_op jit(solution)/shard_map/all_to_all | solution.py:357
  35.3 2.5 %down.1 = f32[4,2048]{1,0:T(4,128)} custom-call(s32[4,16]{1,0:T(4,128)} %far_leaf.3, s32[4]{0:T(128)} %far_count.3, f32[4,2048]{1,0:T(4,128)S(1)} %get-tuple-element.21.base, bf16[256,64]{1,0:T(8,128)(2,1)S(1)} %get-tuple-element.22.down_high, bf16[256,64]{1,0:T(8,128)(2,1)S(1)} %get-tuple-element.23.down_low, ...), custom_call_target="tpu_custom_call" | custom-call | tf_op jit(solution)/shard_map/down/pallas_call | solution.py:388
Async XLA Ops:
  2.3 21.0 %all-to-all-start = ((f32[32,4,384]{2,1,0:T(4,128)}), f32[32,4,384]{2,1,0:T(4,128)S(1)}, u32[]{:S(2)}, u32[]{:S(2)}) async-start(f32[32,4,384]{2,1,0:T(4,128)} %up.1), calls=%async_computation | async-start | bytes 393216 | tf_op jit(solution)/shard_map/all_to_all | solution.py:322
  14.9 7.1 %collective-permute-start = (bf16[4,2048]{1,0:T(4,128)(2,1)}, bf16[4,2048]{1,0:T(4,128)(2,1)S(1)}, u32[]{:S(2)}, u32[]{:S(2)}) collective-permute-start(bf16[4,2048]{1,0:T(4,128)(2,1)} %src.1), channel_id=1, source_target_pairs={{1,2},{3,4},{5,6},{7,8},{9,10},{11,12},{13,14},{15,16},{17,18},{19... | collective-permute-start | bytes 49160 | tf_op jit(solution)/shard_map/ppermute | solution.py:272
  16.1 5.9 %collective-permute-start.1 = (bf16[4,2048]{1,0:T(4,128)(2,1)}, bf16[4,2048]{1,0:T(4,128)(2,1)S(1)}, u32[]{:S(2)}, u32[]{:S(2)}) collective-permute-start(bf16[4,2048]{1,0:T(4,128)(2,1)} %src.1), channel_id=1, source_target_pairs={{0,1},{2,3},{4,5},{6,7},{8,9},{10,11},{12,13},{14,15},{16,17},{18,... | collective-permute-start | bytes 49160 | tf_op jit(solution)/shard_map/ppermute | solution.py:272
  24.1 11.2 %all-to-all-start.1 = ((f32[8,4,640]{2,1,0:T(4,128)}), f32[8,4,640]{2,1,0:T(4,128)S(1)}, u32[]{:S(2)}, u32[]{:S(2)}) async-start(f32[8,4,640]{2,1,0:T(4,128)} %group.1), calls=%async_computation.1 | async-start | bytes 163840 | tf_op jit(solution)/shard_map/all_to_all | solution.py:357
where the time goes:
time: 38.3 us; the launch traced here: 37.8 us
  starting transfers between devices  21.3 us (56%)
  Pallas kernels  13.9 us (36%)
  waiting for transfers between devices  2.5 us (7%)
    all_to_all x1, starting transfers between devices, per_device(): first = lax.all_to_all(send, 'dev', 0, 0, axis_index_groups=[turned])  12.6 us
    all_to_all x1, starting transfers between devices, per_device(): second = lax.all_to_all(send, 'grp', 0, 0)  6.31 us
    pallas_call x1, Pallas kernels, per_device(): pl.pallas_call(mid_kernel, out_shape=[sds(sources.shape, F32), sds((WIDE,...  4.01 us
    pallas_call x1, Pallas kernels, per_device(): pl.pallas_call(own_kernel, out_shape=[sds(sources.shape, F32), sds(neighb...  3.03 us
    pallas_call x1, Pallas kernels, per_device(): pl.pallas_call(down_kernel, out_shape=sds(sources.shape, F32), in_specs=[...  2.49 us
    ppermute x2, starting transfers between devices, swapped(): lax.ppermute(value, ('grp', 'dev'), pairs + [(j, i) for i, j in pairs])  2.45 us
    pallas_call x1, Pallas kernels, per_device(): pl.pallas_call(up_kernel, out_shape=sds((n_dev, NVEC, 2 * RANK + WIDE), F...  2.34 us
    ppermute x2, waiting for transfers between devices, swapped(): lax.ppermute(value, ('grp', 'dev'), pairs + [(j, i) for i, j in pairs])  1.58 us
  transfers between devices with their start and end apart: 4, of which 2 were waited for; matrix products, arithmetic and copies ran while one was open for 0% of the time, Pallas kernels for 22%

commit v1 on v0

--- a/solution.py
+++ b/solution.py
@@ -13,6 +13,7 @@
 NVEC = 4
 LPD = 4
 FARW = 3
+GRP_TURN = 2
 TURN = 31
 WIDE = LPD * RANK
 VMEM = pl.BlockSpec(memory_space=pltpu.VMEM)
@@ -77,10 +78,10 @@
         pltpu.make_async_copy(a, b, sem.at[i])
         for i, (a, b) in enumerate(
             (
+                (src_h, src),
+                (bases_h, bases),
                 (leaf_h, leaf),
                 (cluster_h, cluster),
-                (src_h, src),
-                (bases_h, bases),
             )
         )
     ]
@@ -88,13 +89,13 @@
         c.start()
     copies[0].wait()
     copies[1].wait()
-    to_cluster = two_parts(leaf[...].reshape(WIDE, RANK))
-    to_group = two_parts(cluster[0])
-    copies[2].wait()
-    copies[3].wait()
     every = jnp.concatenate(
         [rows_by_rows(src[:, l * LEAF : (l + 1) * LEAF], bases[l]) for l in range(LPD)], axis=1
     )
+    copies[2].wait()
+    to_cluster = two_parts(leaf[...].reshape(WIDE, RANK))
+    copies[3].wait()
+    to_group = two_parts(cluster[0])
     cluster_rows = close_dot(jnp.concatenate([every, jnp.zeros_like(every)], axis=0), to_cluster)
     group_rows = close_dot(cluster_rows, to_group)
     row = jnp.concatenate([cluster_rows[:NVEC], group_rows[:NVEC], every], axis=1)
@@ -233,14 +234,15 @@
     sums = no_sums()
     for h in range(n_grp):
         c = tiles(top_coupling[0, h])
-        x = jnp.where(h != g, second[h, :, RANK : 2 * RANK], 0.0)
+        x = second[(h - GRP_TURN) % n_grp, :, RANK : 2 * RANK]
+        x = jnp.where(h != g, x, 0.0)
         for v in range(NVEC):
             sums[v] = sums[v] + c * spread(x, v)[None]
     parts = parts_of(jnp.transpose(lanes_to_matrix(sums))[:8])
     field = rows_by_rows(parts, down_high[...])
     field = field[:8] + field[8:16] + field[16:24] + rows_by_rows(parts[:16], down_low[...])[:8]
 
-    side = (g + jnp.where(d < FARW, -1, 1)) & (n_grp - 1)
+    side = (g + jnp.where(d < FARW, -1, 1) - GRP_TURN) & (n_grp - 1)
     for k in range(2):
         start = 2 * RANK + k * WIDE
         fill(table, k * LPD, second[side, :, start : start + WIDE])
@@ -354,7 +356,8 @@
         compiler_params=params(4),
         name="group",
     )(first)
-    second = lax.all_to_all(send, "grp", 0, 0)
+    turned = [(i + GRP_TURN) % n_grp for i in range(n_grp)]
+    second = lax.all_to_all(send, "grp", 0, 0, axis_index_groups=[turned])
     base, down_high, down_low, bases_v, coupling_v, top_v = pl.pallas_call(
         mid_kernel,
         out_shape=[

time: 38.3 us -> 37.7 us (0.984)
  waiting for transfers between devices: 2.5 us -> 1.79 us
    all_to_all x1, waiting for transfers between devices: 0.92 us -> 0.2 us  [per_device(): second = lax.all_to_all(send, 'grp', 0, 0, axis_index_groups=[turned])]
  transfers between devices with their start and end apart: 4 -> 4, of which waited for: 2 -> 2; matrix products, arithmetic and copies ran while one was open for 0% -> 0% of each run, Pallas kernels for 22% -> 23%
where the time goes in v1:
time: 37.7 us; the launch traced here: 37.1 us
  starting transfers between devices  21.4 us (57%)
  Pallas kernels  13.9 us (37%)
  waiting for transfers between devices  1.79 us (5%)
    all_to_all x1, starting transfers between devices, per_device(): first = lax.all_to_all(send, 'dev', 0, 0, axis_index_groups=[turned])  12.6 us
    all_to_all x1, starting transfers between devices, per_device(): second = lax.all_to_all(send, 'grp', 0, 0, axis_index_groups=[turned])  6.37 us
    pallas_call x1, Pallas kernels, per_device(): pl.pallas_call(mid_kernel, out_shape=[sds(sources.shape, F32), sds((WIDE,...  4.01 us
    pallas_call x1, Pallas kernels, per_device(): pl.pallas_call(own_kernel, out_shape=[sds(sources.shape, F32), sds(neighb...  3.03 us
    pallas_call x1, Pallas kernels, per_device(): pl.pallas_call(down_kernel, out_shape=sds(sources.shape, F32), in_specs=[...  2.48 us
    ppermute x2, starting transfers between devices, swapped(): lax.ppermute(value, ('grp', 'dev'), pairs + [(j, i) for i, j in pairs])  2.45 us
    pallas_call x1, Pallas kernels, per_device(): pl.pallas_call(up_kernel, out_shape=sds((n_dev, NVEC, 2 * RANK + WIDE), F...  2.27 us
    ppermute x2, waiting for transfers between devices, swapped(): lax.ppermute(value, ('grp', 'dev'), pairs + [(j, i) for i, j in pairs])  1.58 us
  transfers between devices with their start and end apart: 4, of which 2 were waited for; matrix products, arithmetic and copies ran while one was open for 0% of the time, Pallas kernels for 23%

profile of v1, /device:TPU:1, one launch (start us, length us, event | category | flops | bytes accessed | tf_op | source)
XLA Modules:
  0.0 37.1 jit_solution(10950890586400218731)
XLA Ops:
  0.0 2.3 %up.1 = f32[32,4,384]{2,1,0:T(4,128)} custom-call(bf16[4,2048]{1,0:T(4,128)(2,1)} %src.1, bf16[4,64,512]{2,1,0:T(8,128)(2,1)} %bases_h.3, f32[4,64,64]{2,1,0:T(8,128)} %leaf_h.3, f32[1,64,64]{2,1,0:T(8,128)} %transfer_h.1), custom_call_target="tpu_custom_call" | custom-call | tf_op jit(solution)/shard_map/up/pallas_call | solution.py:308
  2.3 12.6 %all-to-all-start = ((f32[32,4,384]{2,1,0:T(4,128)}), f32[32,4,384]{2,1,0:T(4,128)S(1)}, u32[]{:S(2)}, u32[]{:S(2)}) async-start(f32[32,4,384]{2,1,0:T(4,128)} %up.1), calls=%async_computation | async-start | bytes 393216 | tf_op jit(solution)/shard_map/all_to_all | solution.py:324
  14.9 1.2 %collective-permute-start = (bf16[4,2048]{1,0:T(4,128)(2,1)}, bf16[4,2048]{1,0:T(4,128)(2,1)S(1)}, u32[]{:S(2)}, u32[]{:S(2)}) collective-permute-start(bf16[4,2048]{1,0:T(4,128)(2,1)} %src.1), channel_id=1, source_target_pairs={{1,2},{3,4},{5,6},{7,8},{9,10},{11,12},{13,14},{15,16},{17,18},{19... | collective-permute-start | bytes 49160 | tf_op jit(solution)/shard_map/ppermute | solution.py:274
  16.0 1.3 %collective-permute-start.1 = (bf16[4,2048]{1,0:T(4,128)(2,1)}, bf16[4,2048]{1,0:T(4,128)(2,1)S(1)}, u32[]{:S(2)}, u32[]{:S(2)}) collective-permute-start(bf16[4,2048]{1,0:T(4,128)(2,1)} %src.1), channel_id=1, source_target_pairs={{0,1},{2,3},{4,5},{6,7},{8,9},{10,11},{12,13},{14,15},{16,17},{18,... | collective-permute-start | bytes 49160 | tf_op jit(solution)/shard_map/ppermute | solution.py:274
  17.3 3.0 %own.1 = (f32[4,2048]{1,0:T(4,128)S(1)}, bf16[4,512,512]{2,1,0:T(8,128)(2,1)S(1)}) custom-call(bf16[4,2048]{1,0:T(4,128)(2,1)} %src.1, bf16[4,512,512]{2,1,0:T(8,128)(2,1)} %self_h.1, bf16[4,512,512]{2,1,0:T(8,128)(2,1)} %other_h.1), custom_call_target="tpu_custom_call" | custom-call | flops 20000000 | bytes 4000000 | tf_op jit(solution)/shard_map/own/pallas_call | solution.py:328
  20.4 1.6 %collective-permute-done.even_swap = bf16[4,2048]{1,0:T(4,128)(2,1)S(1)} collective-permute-done((bf16[4,2048]{1,0:T(4,128)(2,1)}, bf16[4,2048]{1,0:T(4,128)(2,1)S(1)}, u32[]{:S(2)}, u32[]{:S(2)}) %collective-permute-start) | collective-permute-done | bytes 16416 | tf_op jit(solution)/shard_map/ppermute | solution.py:274
  22.0 0.0 collective-permute-done.1.odd_swap
  22.0 1.4 %near.1 = f32[4,2048]{1,0:T(4,128)S(1)} custom-call(s32[4]{0:T(128)} %near_list.1, bf16[4,2048]{1,0:T(4,128)(2,1)} %src.1, bf16[4,2048]{1,0:T(4,128)(2,1)S(1)} %collective-permute-done.even_swap, bf16[4,2048]{1,0:T(4,128)(2,1)S(1)} %collective-permute-done.1.odd_swap, f32[4,2048]{1,0:T(4,128)S(1)} %get-tuple-element.17.own, ...), custom_call_target="tpu_custom_call" | custom-call | flops 20000000 | bytes 2000000 | tf_op jit(solution)/shard_map/near/pallas_call | solution.py:341
  23.3 0.0 all-to-all-done.first
  23.3 0.7 %group.1 = f32[8,4,640]{2,1,0:T(4,128)} custom-call(f32[32,4,384]{2,1,0:T(4,128)S(1)} %all-to-all-done.first), custom_call_target="tpu_custom_call" | custom-call | tf_op jit(solution)/shard_map/group/pallas_call | solution.py:351
  24.0 6.4 %all-to-all-start.1 = ((f32[8,4,640]{2,1,0:T(4,128)}), f32[8,4,640]{2,1,0:T(4,128)S(1)}, u32[]{:S(2)}, u32[]{:S(2)}) async-start(f32[8,4,640]{2,1,0:T(4,128)} %group.1), calls=%async_computation.1 | async-start | bytes 163840 | tf_op jit(solution)/shard_map/all_to_all | solution.py:360
  30.4 4.0 %mid.1 = (f32[4,2048]{1,0:T(4,128)S(1)}, bf16[256,64]{1,0:T(8,128)(2,1)S(1)}, bf16[256,64]{1,0:T(8,128)(2,1)S(1)}, bf16[4,64,512]{2,1,0:T(8,128)(2,1)S(1)}, f32[...) custom-call(s32[4,16]{1,0:T(4,128)} %far_leaf.3, s32[4]{0:T(128)} %far_count.3, s32[1,8]{1,0:T(1,128)} %far_cluster.1, ...), custom_call_target="tpu_custom_call" | custom-call | flops 40000000 | bytes 5000000 | tf_op jit(solution)/shard_map/mid/pallas_call | solution.py:361
  34.4 0.2 all-to-all-done.1.second
  34.6 2.5 %down.1 = f32[4,2048]{1,0:T(4,128)} custom-call(s32[4,16]{1,0:T(4,128)} %far_leaf.3, s32[4]{0:T(128)} %far_count.3, f32[4,2048]{1,0:T(4,128)S(1)} %get-tuple-element.21.base, bf16[256,64]{1,0:T(8,128)(2,1)S(1)} %get-tuple-element.22.down_high, bf16[256,64]{1,0:T(8,128)(2,1)S(1)} %get-tuple-element.23.down_low, ...), custom_call_target="tpu_custom_call" | custom-call | tf_op jit(solution)/shard_map/down/pallas_call | solution.py:391
Async XLA Ops:
  2.3 21.0 %all-to-all-start = ((f32[32,4,384]{2,1,0:T(4,128)}), f32[32,4,384]{2,1,0:T(4,128)S(1)}, u32[]{:S(2)}, u32[]{:S(2)}) async-start(f32[32,4,384]{2,1,0:T(4,128)} %up.1), calls=%async_computation | async-start | bytes 393216 | tf_op jit(solution)/shard_map/all_to_all | solution.py:324
  14.9 7.1 %collective-permute-start = (bf16[4,2048]{1,0:T(4,128)(2,1)}, bf16[4,2048]{1,0:T(4,128)(2,1)S(1)}, u32[]{:S(2)}, u32[]{:S(2)}) collective-permute-start(bf16[4,2048]{1,0:T(4,128)(2,1)} %src.1), channel_id=1, source_target_pairs={{1,2},{3,4},{5,6},{7,8},{9,10},{11,12},{13,14},{15,16},{17,18},{19... | collective-permute-start | bytes 49160 | tf_op jit(solution)/shard_map/ppermute | solution.py:274
  16.0 5.9 %collective-permute-start.1 = (bf16[4,2048]{1,0:T(4,128)(2,1)}, bf16[4,2048]{1,0:T(4,128)(2,1)S(1)}, u32[]{:S(2)}, u32[]{:S(2)}) collective-permute-start(bf16[4,2048]{1,0:T(4,128)(2,1)} %src.1), channel_id=1, source_target_pairs={{0,1},{2,3},{4,5},{6,7},{8,9},{10,11},{12,13},{14,15},{16,17},{18,... | collective-permute-start | bytes 49160 | tf_op jit(solution)/shard_map/ppermute | solution.py:274
  24.0 10.6 %all-to-all-start.1 = ((f32[8,4,640]{2,1,0:T(4,128)}), f32[8,4,640]{2,1,0:T(4,128)S(1)}, u32[]{:S(2)}, u32[]{:S(2)}) async-start(f32[8,4,640]{2,1,0:T(4,128)} %group.1), calls=%async_computation.1 | async-start | bytes 163840 | tf_op jit(solution)/shard_map/all_to_all | solution.py:360

commit v2 on v1

--- a/solution.py
+++ b/solution.py
@@ -13,8 +13,8 @@
 NVEC = 4
 LPD = 4
 FARW = 3
-GRP_TURN = 2
-TURN = 31
+GRP_TURN = 3
+TURN = 15
 WIDE = LPD * RANK
 VMEM = pl.BlockSpec(memory_space=pltpu.VMEM)
 HBM = pl.BlockSpec(memory_space=pltpu.HBM)
@@ -27,8 +27,14 @@
     )
 
 
-def exact_dot(a, b):
-    return jnp.dot(a, b, precision=HIGH, preferred_element_type=F32)
+def split_dot(a, b):
+    a_high, a_low = two_parts(a)
+    b_high, b_low = two_parts(b)
+    return (
+        jnp.dot(a_high, b_high, preferred_element_type=F32)
+        + jnp.dot(a_high, b_low, preferred_element_type=F32)
+        + jnp.dot(a_low, b_high, preferred_element_type=F32)
+    )
 
 
 def parts_of(rows):
@@ -188,7 +194,7 @@
     for c in copies[:3]:
         c.wait()
     to_cluster = leaf_transfer[...].reshape(WIDE, RANK)
-    to_group = exact_dot(to_cluster, transfer[0])
+    to_group = split_dot(to_cluster, transfer[0])
     high = to_group.astype(BF16)
     down_high[...] = high
     down_low[...] = (to_group - high.astype(F32)).astype(BF16)
@@ -198,7 +204,7 @@
         x = first[(far_cluster[0, s] - TURN) & (n_dev - 1), :, :RANK]
         for v in range(NVEC):
             sums[v] = sums[v] + c * spread(x, v)[None]
-    from_cluster = exact_dot(to_cluster, lanes_to_matrix(sums))
+    from_cluster = split_dot(to_cluster, lanes_to_matrix(sums))
 
     def entry(l, s):
         leaf = far_leaf[l, s]

time: 37.7 us -> 37.3 us (0.989)
  waiting for transfers between devices: 1.79 us -> 1.23 us
    ppermute x2, starting transfers between devices: 2.45 us -> 3.6 us  [swapped(): lax.ppermute(value, ('grp', 'dev'), pairs + [(j, i) for i, j in pairs])]
    ppermute x2, waiting for transfers between devices: 1.58 us -> 0.9 us  [swapped(): lax.ppermute(value, ('grp', 'dev'), pairs + [(j, i) for i, j in pairs])]
    all_to_all x1, starting transfers between devices: 6.37 us -> 5.9 us  [per_device(): second = lax.all_to_all(send, 'grp', 0, 0, axis_index_groups=[turned])]
where the time goes in v2:
time: 37.3 us; the launch traced here: 36.7 us
  starting transfers between devices  21.7 us (58%)
  Pallas kernels  13.8 us (37%)
  waiting for transfers between devices  1.23 us (3%)
    all_to_all x1, starting transfers between devices, per_device(): first = lax.all_to_all(send, 'dev', 0, 0, axis_index_groups=[turned])  12.2 us
    all_to_all x1, starting transfers between devices, per_device(): second = lax.all_to_all(send, 'grp', 0, 0, axis_index_groups=[turned])  5.9 us
    pallas_call x1, Pallas kernels, per_device(): pl.pallas_call(mid_kernel, out_shape=[sds(sources.shape, F32), sds((WIDE,...  3.87 us
    ppermute x2, starting transfers between devices, swapped(): lax.ppermute(value, ('grp', 'dev'), pairs + [(j, i) for i, j in pairs])  3.6 us
    pallas_call x1, Pallas kernels, per_device(): pl.pallas_call(own_kernel, out_shape=[sds(sources.shape, F32), sds(neighb...  3.07 us
    pallas_call x1, Pallas kernels, per_device(): pl.pallas_call(down_kernel, out_shape=sds(sources.shape, F32), in_specs=[...  2.48 us
    pallas_call x1, Pallas kernels, per_device(): pl.pallas_call(up_kernel, out_shape=sds((n_dev, NVEC, 2 * RANK + WIDE), F...  2.27 us
    pallas_call x1, Pallas kernels, per_device(): pl.pallas_call(near_kernel, out_shape=sds(sources.shape, F32), in_specs=[...  1.37 us
  transfers between devices with their start and end apart: 4, of which 2 were waited for; matrix products, arithmetic and copies ran while one was open for 0% of the time, Pallas kernels for 23%

profile of v2, /device:TPU:1, one launch (start us, length us, event | category | flops | bytes accessed | tf_op | source)
XLA Modules:
  0.0 36.7 jit_solution(15314004566095352427)
XLA Ops:
  0.0 2.3 %up.1 = f32[32,4,384]{2,1,0:T(4,128)} custom-call(bf16[4,2048]{1,0:T(4,128)(2,1)} %src.1, bf16[4,64,512]{2,1,0:T(8,128)(2,1)} %bases_h.3, f32[4,64,64]{2,1,0:T(8,128)} %leaf_h.3, f32[1,64,64]{2,1,0:T(8,128)} %transfer_h.1), custom_call_target="tpu_custom_call" | custom-call | tf_op jit(solution)/shard_map/up/pallas_call | solution.py:314
  2.3 12.2 %all-to-all-start = ((f32[32,4,384]{2,1,0:T(4,128)}), f32[32,4,384]{2,1,0:T(4,128)S(1)}, u32[]{:S(2)}, u32[]{:S(2)}) async-start(f32[32,4,384]{2,1,0:T(4,128)} %up.1), calls=%async_computation | async-start | bytes 393216 | tf_op jit(solution)/shard_map/all_to_all | solution.py:330
  14.5 3.6 %collective-permute-start = (bf16[4,2048]{1,0:T(4,128)(2,1)}, bf16[4,2048]{1,0:T(4,128)(2,1)S(1)}, u32[]{:S(2)}, u32[]{:S(2)}) collective-permute-start(bf16[4,2048]{1,0:T(4,128)(2,1)} %src.1), channel_id=1, source_target_pairs={{1,2},{3,4},{5,6},{7,8},{9,10},{11,12},{13,14},{15,16},{17,18},{19... | collective-permute-start | bytes 49160 | tf_op jit(solution)/shard_map/ppermute | solution.py:280
  18.1 0.0 collective-permute-start.1
  18.1 3.1 %own.1 = (f32[4,2048]{1,0:T(4,128)S(1)}, bf16[4,512,512]{2,1,0:T(8,128)(2,1)S(1)}) custom-call(bf16[4,2048]{1,0:T(4,128)(2,1)} %src.1, bf16[4,512,512]{2,1,0:T(8,128)(2,1)} %self_h.1, bf16[4,512,512]{2,1,0:T(8,128)(2,1)} %other_h.1), custom_call_target="tpu_custom_call" | custom-call | flops 20000000 | bytes 4000000 | tf_op jit(solution)/shard_map/own/pallas_call | solution.py:334
  21.2 0.9 %collective-permute-done.even_swap = bf16[4,2048]{1,0:T(4,128)(2,1)S(1)} collective-permute-done((bf16[4,2048]{1,0:T(4,128)(2,1)}, bf16[4,2048]{1,0:T(4,128)(2,1)S(1)}, u32[]{:S(2)}, u32[]{:S(2)}) %collective-permute-start) | collective-permute-done | bytes 16416 | tf_op jit(solution)/shard_map/ppermute | solution.py:280
  22.1 0.0 collective-permute-done.1.odd_swap
  22.1 1.4 %near.1 = f32[4,2048]{1,0:T(4,128)S(1)} custom-call(s32[4]{0:T(128)} %near_list.1, bf16[4,2048]{1,0:T(4,128)(2,1)} %src.1, bf16[4,2048]{1,0:T(4,128)(2,1)S(1)} %collective-permute-done.even_swap, bf16[4,2048]{1,0:T(4,128)(2,1)S(1)} %collective-permute-done.1.odd_swap, f32[4,2048]{1,0:T(4,128)S(1)} %get-tuple-element.17.own, ...), custom_call_target="tpu_custom_call" | custom-call | flops 20000000 | bytes 2000000 | tf_op jit(solution)/shard_map/near/pallas_call | solution.py:347
  23.4 0.0 all-to-all-done.first
  23.5 0.7 %group.1 = f32[8,4,640]{2,1,0:T(4,128)} custom-call(f32[32,4,384]{2,1,0:T(4,128)S(1)} %all-to-all-done.first), custom_call_target="tpu_custom_call" | custom-call | tf_op jit(solution)/shard_map/group/pallas_call | solution.py:357
  24.1 5.9 %all-to-all-start.1 = ((f32[8,4,640]{2,1,0:T(4,128)}), f32[8,4,640]{2,1,0:T(4,128)S(1)}, u32[]{:S(2)}, u32[]{:S(2)}) async-start(f32[8,4,640]{2,1,0:T(4,128)} %group.1), calls=%async_computation.1 | async-start | bytes 163840 | tf_op jit(solution)/shard_map/all_to_all | solution.py:366
  30.0 3.9 %mid.1 = (f32[4,2048]{1,0:T(4,128)S(1)}, bf16[256,64]{1,0:T(8,128)(2,1)S(1)}, bf16[256,64]{1,0:T(8,128)(2,1)S(1)}, bf16[4,64,512]{2,1,0:T(8,128)(2,1)S(1)}, f32[...) custom-call(s32[4,16]{1,0:T(4,128)} %far_leaf.3, s32[4]{0:T(128)} %far_count.3, s32[1,8]{1,0:T(1,128)} %far_cluster.1, ...), custom_call_target="tpu_custom_call" | custom-call | flops 40000000 | bytes 5000000 | tf_op jit(solution)/shard_map/mid/pallas_call | solution.py:367
  33.9 0.3 all-to-all-done.1.second
  34.3 2.5 %down.1 = f32[4,2048]{1,0:T(4,128)} custom-call(s32[4,16]{1,0:T(4,128)} %far_leaf.3, s32[4]{0:T(128)} %far_count.3, f32[4,2048]{1,0:T(4,128)S(1)} %get-tuple-element.21.base, bf16[256,64]{1,0:T(8,128)(2,1)S(1)} %get-tuple-element.22.down_high, bf16[256,64]{1,0:T(8,128)(2,1)S(1)} %get-tuple-element.23.down_low, ...), custom_call_target="tpu_custom_call" | custom-call | tf_op jit(solution)/shard_map/down/pallas_call | solution.py:397
Async XLA Ops:
  2.3 21.2 %all-to-all-start = ((f32[32,4,384]{2,1,0:T(4,128)}), f32[32,4,384]{2,1,0:T(4,128)S(1)}, u32[]{:S(2)}, u32[]{:S(2)}) async-start(f32[32,4,384]{2,1,0:T(4,128)} %up.1), calls=%async_computation | async-start | bytes 393216 | tf_op jit(solution)/shard_map/all_to_all | solution.py:330
  14.5 7.6 %collective-permute-start = (bf16[4,2048]{1,0:T(4,128)(2,1)}, bf16[4,2048]{1,0:T(4,128)(2,1)S(1)}, u32[]{:S(2)}, u32[]{:S(2)}) collective-permute-start(bf16[4,2048]{1,0:T(4,128)(2,1)} %src.1), channel_id=1, source_target_pairs={{1,2},{3,4},{5,6},{7,8},{9,10},{11,12},{13,14},{15,16},{17,18},{19... | collective-permute-start | bytes 49160 | tf_op jit(solution)/shard_map/ppermute | solution.py:280
  18.1 4.0 %collective-permute-start.1 = (bf16[4,2048]{1,0:T(4,128)(2,1)}, bf16[4,2048]{1,0:T(4,128)(2,1)S(1)}, u32[]{:S(2)}, u32[]{:S(2)}) collective-permute-start(bf16[4,2048]{1,0:T(4,128)(2,1)} %src.1), channel_id=1, source_target_pairs={{0,1},{2,3},{4,5},{6,7},{8,9},{10,11},{12,13},{14,15},{16,17},{18,... | collective-permute-start | bytes 49160 | tf_op jit(solution)/shard_map/ppermute | solution.py:280
  24.1 10.1 %all-to-all-start.1 = ((f32[8,4,640]{2,1,0:T(4,128)}), f32[8,4,640]{2,1,0:T(4,128)S(1)}, u32[]{:S(2)}, u32[]{:S(2)}) async-start(f32[8,4,640]{2,1,0:T(4,128)} %group.1), calls=%async_computation.1 | async-start | bytes 163840 | tf_op jit(solution)/shard_map/all_to_all | solution.py:366
